TPU v7x, 256 devices: a whole 4x4x8 slice. The times are simulated.
256 devices in a mesh: row: 16 (over x, z_hi), col: 16 (over y, z_lo, core).
Axes of the slice: x: 4, y: 4, z: 8 (z_hi: 4, z_lo: 2; z = z_hi * 2 + z_lo), core: 2. Of those that a mesh axis runs over, the one named last changes fastest.
Arguments:
- gradient: bfloat16 [8192, 28672], P('row', 'col')
Outputs:
- left_gram: float32 [8192, 2048], P('row', 'col')
- right_gram: float32 [28672, 1792], P(('col', 'row'))
All inputs are finite; a program needn't handle non-finite values.
Results may differ from a plain program's by a relative error of at most 0.0003.
Values may be sent and summed in bfloat16 or wider, within the bound.
No kernel may reach another device: no remote copies, remote signals or barrier semaphores. Data moves between devices by JAX's collectives and lax.ppermute only.
A program may use at most 64 MiB of HBM per device.

v0:
```python
import jax
import jax.numpy as jnp
from jax import lax
from jax.sharding import PartitionSpec as P

LBLK = 2048


def partner(array, axis, stride):
    return lax.ppermute(array, axis, [(i, i ^ 1 << stride) for i in range(lax.axis_size(axis))])


def outer_rows(left, right):
    return lax.dot_general(
        left, right, (((1,), (1,)), ((), ())), preferred_element_type=jnp.float32
    )


def shards(gradient):
    rows = gradient.shape[0]
    group = LBLK // rows
    block = gradient
    index = lax.axis_index("row")
    for bit in range(group.bit_length() - 1):
        other = partner(block, "row", bit)
        upper = index >> bit & 1 == 1
        lower_half = jnp.where(upper, other, block)
        upper_half = jnp.where(upper, block, other)
        block = jnp.concatenate([lower_half, upper_half], axis=0)
    partial_value = outer_rows(gradient, block)
    total_cols = gradient.shape[1] * lax.axis_size("col")
    summed = lax.psum(partial_value, "col")
    width = LBLK // lax.axis_size("col")
    left_gram = lax.dynamic_slice_in_dim(summed, lax.axis_index("col") * width, width, 1) * (
        1.0 / total_cols
    )
    total_rows = rows * lax.axis_size("row")
    right_gram = lax.psum_scatter(
        lax.dot_general(
            gradient, gradient, (((0,), (0,)), ((), ())), preferred_element_type=jnp.float32
        ),
        "row",
        scatter_dimension=0,
        tiled=True,
    ) * (1.0 / total_rows)
    return (left_gram, right_gram)


def solution(mesh):
    in_specs = (P("row", "col"),)
    out_specs = (P("row", "col"), P(("col", "row"), None))
    return jax.shard_map(shards, mesh=mesh, in_specs=in_specs, out_specs=out_specs, check_vma=False)
```

profile of v0, /device:TPU:25, one launch (start us, length us, event | category | flops | bytes accessed | tf_op | source)
XLA Modules:
  0.0 531.3 jit_solution(14040443319717663407)
XLA Ops:
  8.0 0.0 all-reduce.2.cloned.1.call-start
  8.0 3.1 collective-permute-start
  11.1 79.4 %collective-permute-done = bf16[512,1792]{1,0:T(8,128)(2,1)} collective-permute-done((bf16[512,1792]{1,0:T(8,128)(2,1)}, bf16[512,1792]{1,0:T(8,128)(2,1)}, u32[]{:S(2)}, u32[]{:S(2)}) %collective-permute-start) | collective-permute-done | bytes 1835040 | tf_op jit(solution)/shard_map/ppermute | solution.py:10
  90.5 2.3 broadcast_select_fusion.3
  92.8 0.0 copy-start
  92.8 2.2 pad_maximum_fusion
  95.0 0.2 copy-done
  95.3 6.5 %collective-permute-start.1 = (bf16[1024,1792]{1,0:T(8,128)(2,1)}, bf16[1024,1792]{1,0:T(8,128)(2,1)}, u32[]{:S(2)}, u32[]{:S(2)}) collective-permute-start(bf16[1024,1792]{1,0:T(8,128)(2,1)} %pad_maximum_fusion), channel_id=1, source_target_pairs={{0,32},{16,48},{32,0},{48,16},{64,96},{80,112},{96,64},{112,80},{1... | collective-permute-start | bytes 11010056 | tf_op jit(solution)/shard_map/ppermute | solution.py:10
  101.8 0.0 copy-start.1
  101.8 158.5 %collective-permute-done.1 = bf16[1024,1792]{1,0:T(8,128)(2,1)} collective-permute-done((bf16[1024,1792]{1,0:T(8,128)(2,1)}, bf16[1024,1792]{1,0:T(8,128)(2,1)}, u32[]{:S(2)}, u32[]{:S(2)}) %collective-permute-start.1) | collective-permute-done | bytes 3670048 | tf_op jit(solution)/shard_map/ppermute | solution.py:10
  260.3 3.3 broadcast_select_fusion.1
  263.5 0.0 copy-done.1
  263.6 7.0 %fusion.4 = f32[512,2048]{0,1:T(8,128)} fusion(bf16[512,1792]{1,0:T(8,128)(2,1)S(1)} %copy-done.1, bf16[1024,1792]{1,0:T(8,128)(2,1)S(1)} %get-tuple-element.5, bf16[1024,1792]{1,0:T(8,128)(2,1)S(1)} %get-tuple-element.4), kind=kOutput, calls=%fused_computation.7 | convolution fusion | flops 3772776448 | bytes 13369344 | tf_op jit(solution)/shard_map/dot_general | solution.py:14
  270.6 0.0 copy-start.2
  270.6 0.0 all-reduce.2.cloned.1.call-update
  270.6 0.0 reduce-scatter.2.cloned.1.call-start
  270.7 1.4 copy-done.2
  272.1 6.5 %fusion.8 = f32[1792,1792]{1,0:T(8,128)} fusion(bf16[512,1792]{1,0:T(8,128)(2,1)S(1)} %copy-done.2), kind=kOutput, calls=%fused_computation.13 | convolution fusion | flops 3288334336 | bytes 14680064 | tf_op jit(solution)/shard_map/dot_general | solution.py:39
  278.6 0.0 reduce-scatter.2.cloned.1.call-update
  278.6 241.3 %all-reduce.2.cloned.1.call-done = f32[512,2048]{0,1:T(8,128)} async-done(((f32[512,2048]{0,1:T(8,128)}), f32[512,2048]{0,1:T(8,128)}) %all-reduce.2.cloned.1.call-update) | async-done | bytes 4194320 | tf_op jit(solution)/shard_map/psum | solution.py:32
  519.9 1.0 dynamic-slice_multiply_fusion
  520.9 0.8 copy.3
  521.8 0.0 reduce-scatter.2.cloned.1.call-done
  521.8 2.1 broadcast_multiply_fusion
Async XLA Ops:
  8.0 511.9 %all-reduce.2.cloned.1.call-start = ((), (), s32[]{:S(2)}) async-start(), calls=%async_computation.1 | async-start | bytes 8388608 | tf_op jit(solution)/shard_map/psum | solution.py:32
  8.0 82.5 %collective-permute-start = (bf16[512,1792]{1,0:T(8,128)(2,1)}, bf16[512,1792]{1,0:T(8,128)(2,1)}, u32[]{:S(2)}, u32[]{:S(2)}) collective-permute-start(bf16[512,1792]{1,0:T(8,128)(2,1)} %param.1), channel_id=1, source_target_pairs={{0,16},{16,0},{32,48},{48,32},{64,80},{80,64},{96,112},{112,96},{1... | collective-permute-start | bytes 5505032 | tf_op jit(solution)/shard_map/ppermute | solution.py:10
  92.8 2.5 copy-start
  95.3 165.0 %collective-permute-start.1 = (bf16[1024,1792]{1,0:T(8,128)(2,1)}, bf16[1024,1792]{1,0:T(8,128)(2,1)}, u32[]{:S(2)}, u32[]{:S(2)}) collective-permute-start(bf16[1024,1792]{1,0:T(8,128)(2,1)} %pad_maximum_fusion), channel_id=1, source_target_pairs={{0,32},{16,48},{32,0},{48,16},{64,96},{80,112},{96,64},{112,80},{1... | collective-permute-start | bytes 11010056 | tf_op jit(solution)/shard_map/ppermute | solution.py:10
  101.8 161.7 %copy-start.1 = (bf16[512,1792]{1,0:T(8,128)(2,1)S(1)}, bf16[512,1792]{1,0:T(8,128)(2,1)}, u32[]{:S(2)}) copy-start(bf16[512,1792]{1,0:T(8,128)(2,1)} %param.1) | copy-start | bytes 5505028
  270.6 1.5 copy-start.2
  270.6 251.1 %reduce-scatter.2.cloned.1.call-start = ((), (), s32[]{:S(2)}) async-start(), calls=%async_computation.2 | async-start | bytes 13647872 | tf_op jit(solution)/shard_map/reduce_scatter | solution.py:38
Sparse Core Ops, SparseCore 0:
  270.7 249.1 all-reduce.1
Sparse Core Ops, SparseCore 1:
  278.7 202.2 reduce-scatter.1
where the time goes:
time: 535 us; the launch traced here: 531 us
  waiting for transfers between devices  479 us (90%)
  between operations  15.5 us (3%)
  matrix products  13.5 us (3%)
  other arithmetic  10.8 us (2%)
  starting transfers between devices  9.7 us (2%)
    psum x1, waiting for transfers between devices, shards(): summed = lax.psum(partial_value, 'col')  241 us
    ppermute x2, waiting for transfers between devices, partner(): lax.ppermute(array, axis, [(i, i ^ 1 << stride) for i in range(lax.axis_s...  238 us
  transfers between devices with their start and end apart: 4, of which 3 were waited for; matrix products, arithmetic and copies ran while one was open for 2% of the time, Pallas kernels for 0%

commit v1 on v0

v1 whole, which is shorter than its diff:
```python
import itertools

import jax
import jax.numpy as jnp
from jax import lax
from jax.sharding import PartitionSpec as P

LBLK = 2048
F32, BF16 = jnp.float32, jnp.bfloat16

SIZES = (4, 4, 4, 2, 2)
PLACES = list(itertools.product(*(range(n) for n in SIZES)))


def number(place):
    x, zh, y, zl, core = (p % n for p, n in zip(place, SIZES))
    return (4 * x + zh) * 16 + 4 * y + 2 * zl + core


def send(array, to):
    return lax.ppermute(array, ("row", "col"), [(number(p), number(to(*p))) for p in PLACES])


POWER = 13
LIFT = 120 / POWER


def inverse_norm(squares):
    return jnp.where(squares > 0, lax.rsqrt(jnp.where(squares > 0, squares, 1.0)), 0.0)


def norm(squares):
    return jnp.sqrt(squares)


def encode(value, rows, cols):
    ratio = value * rows[:, None] * (cols * 2.0**LIFT)[None, :]
    p2 = ratio * ratio
    p4 = p2 * p2
    return (p4 * p4 * (p4 * ratio)).astype(BF16)


def decode(code):
    wide = code.astype(F32)
    size = jnp.exp2(jnp.log2(jnp.abs(wide)) * (1.0 / POWER) - LIFT)
    return jnp.where(wide < 0, -size, size)


def dot(left, right, dim):
    return lax.dot_general(
        left, right, (((dim,), (dim,)), ((), ())), preferred_element_type=F32
    )


def shards(gradient):
    rows, width = gradient.shape
    row, col = lax.axis_index("row"), lax.axis_index("col")
    x, zh = row // 4, row % 4
    y, zl, core = col // 4, col // 2 % 2, col % 2
    total_rows, total_cols = rows * 16, width * 16

    squares = jnp.square(gradient.astype(F32))
    row_squares = jnp.sum(lax.all_gather(jnp.sum(squares, 1), "col"), 0)
    groups = [[4 * a + b for b in range(4)] for a in range(4)]
    row_squares = lax.all_gather(row_squares, "row", axis_index_groups=groups)
    own_squares = jnp.sum(squares, 0)
    col_squares = lax.all_gather(own_squares, "row")

    half = width // 2

    def columns(parity):
        return lax.dynamic_slice_in_dim(gradient, parity * half, half, 1)

    near = send(
        columns((zh + 1) % 2), lambda x, zh, y, zl, core: (x, 2 * core + (zh + 1) % 2, y, zl, zh // 2)
    )
    far = send(columns(zh % 2), lambda x, zh, y, zl, core: (x, 2 * core + zh % 2, y, zl, zh // 2))

    block = width // 4
    inverse_own = inverse_norm(own_squares)
    index = lambda s: (x + s) % 4

    def right_part(s):
        mine = lax.dynamic_slice_in_dim(gradient, index(s) * block, block, 1)
        return dot(mine, gradient, 0)

    right_total = right_part(0)
    right_in = []
    for s in (1, 3, 2):
        scale = lax.dynamic_slice_in_dim(inverse_own, index(s) * block, block, 0)
        code = encode(right_part(s), scale, inverse_own)
        right_in.append((s, send(code, lambda x, zh, y, zl, core: (x + s, zh, y, zl, core))))

    swap = lambda x, zh, y, zl, core: (x, zh, y, zl, 1 - core)
    other_near = send(near, swap)
    other_far = send(far, swap)
    held = jnp.stack([far, near, other_far, other_near])
    place = lambda j: 2 * ((j // 2) ^ core) + (j + zh) % 2
    order = jnp.stack([2 * core + zh % 2, 2 * core + 1 - zh % 2, 2 * (1 - core) + zh % 2, 2 * (1 - core) + 1 - zh % 2])
    held_squares = row_squares[order].reshape(-1)
    flat = held.reshape(LBLK, half)
    inverse_rows = inverse_norm(held_squares)

    def pick(array, j):
        part = lax.dynamic_index_in_dim(array, j, 0, False).reshape(2, 2, 128, *array.shape[2:])
        return lax.dynamic_index_in_dim(part, core, 1, False).reshape(256, *array.shape[2:])

    def left_part(j):
        return dot(flat, pick(held, place(j)), 1)

    left_in = []
    for s in (1, 3, 2):
        j = (y + s) % 4
        code = encode(left_part(j), inverse_rows, inverse_norm(pick(row_squares, j)))
        left_in.append(send(code, lambda x, zh, y, zl, core: (x, zh, y + s, zl, core)))
    left_own = left_part(y)
    left_cols = pick(row_squares, y)
    left_sum = left_own + sum(decode(c) for c in left_in) * (
        norm(held_squares)[:, None] * norm(left_cols)[None, :]
    )

    right_sum = right_total
    for s, code in right_in:
        their = norm(lax.dynamic_index_in_dim(col_squares, (x - s) % 4 * 4 + zh, 0, False))
        mine = lax.dynamic_slice_in_dim(their, x * block, block, 0)
        right_sum = right_sum + decode(code) * mine[:, None] * their[None, :]
    all_squares = jnp.sum(col_squares, 0)
    my_squares = lax.dynamic_slice_in_dim(all_squares, x * block, block, 0)
    right_code = encode(right_sum, inverse_norm(my_squares), inverse_norm(all_squares))
    chunk = block // 4
    right_final = []
    for s in (1, 3, 2):
        piece = lax.dynamic_slice_in_dim(right_code, (zh + s) % 4 * chunk, chunk, 0)
        right_final.append(send(piece, lambda x, zh, y, zl, core: (x, zh + s, y, zl, core)))
    own = lax.dynamic_slice_in_dim(right_sum, zh * chunk, chunk, 0)
    chunk_squares = lax.dynamic_slice_in_dim(my_squares, zh * chunk, chunk, 0)
    right_gram = (
        own + sum(decode(c) for c in right_final) * (norm(chunk_squares)[:, None] * norm(all_squares)[None, :])
    ) * (1.0 / total_rows)

    left_code = encode(left_sum, inverse_rows, inverse_norm(left_cols))

    def final_piece(array, zh_to, zl_to):
        start = place(zh_to) * 512
        return lax.dynamic_slice(array, (start, zl_to * 128), (512, 128))

    left_final = []
    for s in (1, 7, 2, 6, 3, 5, 4):
        z = (2 * zh + zl + s) % 8
        piece = final_piece(left_code, z // 2, z % 2)

        def to(x, zh, y, zl, core):
            z = (2 * zh + zl + s) % 8
            return (x, z // 2, y, z % 2, core)

        left_final.append(send(piece, to))
    mine = final_piece(left_sum, zh, zl)
    out_rows = norm(lax.dynamic_index_in_dim(row_squares, zh, 0, False))
    out_cols = norm(lax.dynamic_slice_in_dim(left_cols, zl * 128, 128, 0))
    left_gram = (mine + sum(decode(c) for c in left_final) * (out_rows[:, None] * out_cols[None, :])) * (
        1.0 / total_cols
    )
    return (left_gram, right_gram)


def solution(mesh):
    in_specs = (P("row", "col"),)
    out_specs = (P("row", "col"), P(("col", "row"), None))
    return jax.shard_map(shards, mesh=mesh, in_specs=in_specs, out_specs=out_specs, check_vma=False)
```

time: 535 us -> 214 us (0.40)
  the two profiles are of different devices: /device:TPU:25 before, /device:TPU:33 now
where the time goes in v1:
time: 214 us; the launch traced here: 213 us
  blocking collectives  81.9 us (38%)
  waiting for transfers between devices  47.1 us (22%)
  starting transfers between devices  40.9 us (19%)
  matrix products  28.6 us (13%)
  other arithmetic  8.63 us (4%)
  local copies, waits for them, and re-layouts  4.8 us (2%)
    ppermute x20, waiting for transfers between devices, send(): lax.ppermute(array, ('row', 'col'), [(number(p), number(to(*p))) for p in...  47.1 us
    ppermute x20, starting transfers between devices, send(): lax.ppermute(array, ('row', 'col'), [(number(p), number(to(*p))) for p in...  40.9 us
    all_gather x1, blocking collectives, shards(): row_squares = jnp.sum(lax.all_gather(jnp.sum(squares, 1), 'col'), 0)  35.5 us
    all_gather x1, blocking collectives, shards(): col_squares = lax.all_gather(own_squares, 'row')  33.9 us
    dot_general x8, matrix products, dot(): lax.dot_general(left, right, (((dim,), (dim,)), ((), ())), preferred_elem...  28.6 us
    all_gather x1, blocking collectives, shards(): row_squares = lax.all_gather(row_squares, 'row', axis_index_groups=groups)  12.4 us
  transfers between devices with their start and end apart: 20, of which 7 were waited for; matrix products, arithmetic and copies ran while one was open for 17% of the time, Pallas kernels for 0%

profile of v1, /device:TPU:33, one launch (start us, length us, event | category | flops | bytes accessed | tf_op | source)
XLA Modules:
  0.0 213.4 jit_solution(17758179092012104219)
XLA Ops:
  0.7 3.0 %constant_dynamic-slice_fusion.27 = (bf16[512,896]{1,0:T(8,128)(2,1)}, bf16[512,896]{1,0:T(8,128)(2,1)}) fusion(bf16[512,1792]{1,0:T(8,128)(2,1)} %param.1, s32[]{:T(128)S(6)} %select_n.576, s32[]{:T(128)S(6)} %select_n.578), kind=kLoop, calls=%fused_computation.216 | loop fusion | bytes 3670024 | tf_op jit(solution)/shard_map/dynamic_slice | solution.py:72
  3.7 5.7 %collective-permute-start.1 = (bf16[512,896]{1,0:T(8,128)(2,1)}, bf16[512,896]{1,0:T(8,128)(2,1)S(1)}, u32[]{:S(2)}, u32[]{:S(2)}) collective-permute-start(bf16[512,896]{1,0:T(8,128)(2,1)} %get-tuple-element.15), channel_id=1, source_target_pairs={{0,16},{1,48},{2,18},{3,50},{4,20},{5,52},{6,22},{7,54},{8,24},{9,... | collective-permute-start | bytes 2752520 | tf_op jit(solution)/shard_map/ppermute | solution.py:21
  9.4 2.8 %collective-permute-start = (bf16[512,896]{1,0:T(8,128)(2,1)}, bf16[512,896]{1,0:T(8,128)(2,1)}, u32[]{:S(2)}, u32[]{:S(2)}) collective-permute-start(bf16[512,896]{1,0:T(8,128)(2,1)} %get-tuple-element.14), channel_id=1, source_target_pairs={{0,0},{1,32},{2,2},{3,34},{4,4},{5,36},{6,6},{7,38},{8,8},{9,40},{... | collective-permute-start | bytes 2752520 | tf_op jit(solution)/shard_map/ppermute | solution.py:21
  12.9 2.8 %multiply_convert_fusion.1 = bf16[448,1792]{1,0:T(8,128)(2,1)} fusion(bf16[512,1792]{1,0:T(8,128)(2,1)S(1)} %copy-done, f32[448]{0:T(512)S(1)} %get-tuple-element.32, f32[1792]{0:T(1024)S(1)} %get-tuple-element.36, s32[]{:T(128)S(6)} %select_n.695), kind=kOutput, calls=%fused_computation.39 | convolution fusion | flops 828506112 | bytes 3975172 | tf_op jit(solution)/shard_map/dot_general | solution.py:50
  15.7 2.7 %collective-permute-start.16 = (bf16[448,1792]{1,0:T(8,128)(2,1)}, bf16[448,1792]{1,0:T(8,128)(2,1)}, u32[]{:S(2)}, u32[]{:S(2)}) collective-permute-start(bf16[448,1792]{1,0:T(8,128)(2,1)} %multiply_convert_fusion.1), channel_id=1, source_target_pairs={{0,128},{1,129},{2,130},{3,131},{4,132},{5,133},{6,134},{7,135},{8... | collective-permute-start | bytes 4816904 | tf_op jit(solution)/shard_map/ppermute | solution.py:21
  18.4 2.7 %multiply_convert_fusion.2 = bf16[448,1792]{1,0:T(8,128)(2,1)} fusion(bf16[512,1792]{1,0:T(8,128)(2,1)S(1)} %copy-done, f32[448]{0:T(512)S(1)} %get-tuple-element.33, f32[1792]{0:T(1024)S(1)} %get-tuple-element.36, s32[]{:T(128)S(6)} %select_n.690), kind=kOutput, calls=%fused_computation.40 | convolution fusion | flops 828506112 | bytes 3975172 | tf_op jit(solution)/shard_map/dot_general | solution.py:50
  22.0 2.8 %multiply_convert_fusion.3 = bf16[448,1792]{1,0:T(8,128)(2,1)} fusion(bf16[512,1792]{1,0:T(8,128)(2,1)S(1)} %copy-done, f32[1792]{0:T(1024)S(1)} %get-tuple-element.36, f32[448]{0:T(512)S(1)} %get-tuple-element.34, s32[]{:T(128)S(6)} %select_n.682), kind=kOutput, calls=%fused_computation.41 | convolution fusion | flops 828506112 | bytes 3975172 | tf_op jit(solution)/shard_map/dot_general | solution.py:50
  25.5 35.5 %all-gather.3 = f32[16,1,512]{2,1,0:T(1,128)S(1)} all-gather(f32[1,1,512]{2,1,0:T(1,128)S(1)} %bitcast.67), channel_id=2, replica_groups=mesh['row'=16,'col'=16] {'col'}, dimensions={0}, use_global_device_ids=true | all-gather | bytes 34816 | tf_op jit(solution)/shard_map/all_gather | solution.py:63
  61.0 12.4 %all-gather.4 = f32[4,1,512]{2,1,0:T(1,128)S(1)} all-gather(f32[1,1,512]{2,1,0:T(1,128)S(1)} %bitcast.66), channel_id=3, replica_groups={{0,16,32,48},{64,80,96,112},{128,144,160,176},{192,208,224,240},{1,17,3..., dimensions={0}, use_global_device_ids=true | all-gather | bytes 10240 | tf_op jit(solution)/shard_map/all_gather | solution.py:65
  73.5 33.9 %all-gather.5 = f32[16,1,1792]{2,1,0:T(1,128)S(1)} all-gather(f32[1,1,1792]{2,1,0:T(1,128)S(1)} %reshape.375), channel_id=4, replica_groups=mesh['row'=16,'col'=16] {'row'}, dimensions={0}, use_global_device_ids=true | all-gather | bytes 121856 | tf_op jit(solution)/shard_map/all_gather | solution.py:67
  108.4 9.7 %collective-permute-start.3 = (bf16[512,896]{1,0:T(8,128)(2,1)S(1)}, bf16[512,896]{1,0:T(8,128)(2,1)}, u32[]{:S(2)}, u32[]{:S(2)}) collective-permute-start(bf16[512,896]{1,0:T(8,128)(2,1)S(1)} %collective-permute-done.1), channel_id=1, source_target_pairs={{0,1},{1,0},{2,3},{3,2},{4,5},{5,4},{6,7},{7,6},{8,9},{9,8},{10,11... | collective-permute-start | bytes 2752520 | tf_op jit(solution)/shard_map/ppermute | solution.py:21
  120.3 1.5 collective-permute-done.2
  121.8 2.0 pad_maximum_fusion
  124.2 1.4 multiply_convert_fusion.5
  125.8 1.4 multiply_convert_fusion.6
  127.3 1.5 collective-permute-start.5
  128.8 1.4 multiply_convert_fusion.7
  130.4 10.1 %multiply_convert_fusion = (bf16[448,1792]{1,0:T(8,128)(2,1)S(1)}, f32[448,1792]{1,0:T(8,128)}) fusion(f32[1792]{0:T(1024)S(1)} %get-tuple-element.31, f32[448]{0:T(512)S(1)} %compare_select_fusion.7, f32[1792]{0:T(1024)S(1)} %get-tuple-element.26, f32[448]{0:T(512)S(1)} %bitcast.78, bf16[448,1792]{1,0:T(8,128)(2,1)} %collective-permute-done.16, ...), kind=kOutput, calls=%fused_computation.38 | convolution fusion | flops 854999040 | bytes 12034052 | tf_op jit(solution)/shard_map/dot_general | solution.py:50
  141.2 3.1 %collective-permute-start.18 = (bf16[112,1792]{1,0:T(8,128)(2,1)S(1)}, bf16[112,1792]{1,0:T(8,128)(2,1)S(1)}, u32[]{:S(2)}, u32[]{:S(2)}) collective-permute-start(bf16[112,1792]{1,0:T(8,128)(2,1)S(1)} %get-tuple-element.17), channel_id=1, source_target_pairs={{0,48},{1,49},{2,50},{3,51},{4,52},{5,53},{6,54},{7,55},{8,56},{9,... | collective-permute-start | bytes 1204232 | tf_op jit(solution)/shard_map/ppermute | solution.py:21
  144.3 7.3 %collective-permute-done.6 = bf16[2048,256]{1,0:T(8,128)(2,1)S(1)} collective-permute-done((bf16[2048,256]{1,0:T(8,128)(2,1)S(1)}, bf16[2048,256]{1,0:T(8,128)(2,1)S(1)}, u32[]{:S(2)}, u32[]{:S(2)}) %collective-permute-start.6) | collective-permute-done | bytes 1048608 | tf_op jit(solution)/shard_map/ppermute | solution.py:21
  151.7 20.6 %collective-permute-done.5 = bf16[2048,256]{1,0:T(8,128)(2,1)S(1)} collective-permute-done((bf16[2048,256]{1,0:T(8,128)(2,1)S(1)}, bf16[2048,256]{1,0:T(8,128)(2,1)S(1)}, u32[]{:S(2)}, u32[]{:S(2)}) %collective-permute-start.5) | collective-permute-done | bytes 1048608 | tf_op jit(solution)/shard_map/ppermute | solution.py:21
  172.2 2.6 %collective-permute-done.4 = bf16[2048,256]{1,0:T(8,128)(2,1)S(1)} collective-permute-done((bf16[2048,256]{1,0:T(8,128)(2,1)S(1)}, bf16[2048,256]{1,0:T(8,128)(2,1)S(1)}, u32[]{:S(2)}, u32[]{:S(2)}) %collective-permute-start.4) | collective-permute-done | bytes 1048608 | tf_op jit(solution)/shard_map/ppermute | solution.py:21
  174.8 5.8 %multiply_convert_fusion.4 = (bf16[2048,256]{1,0:T(8,128)(2,1)S(1)}, f32[2048,256]{1,0:T(8,128)}) fusion(f32[256]{0:T(256)S(1)} %get-tuple-element.44, f32[2048]{0:T(1024)S(1)} %get-tuple-element.43, f32[256]{0:T(256)S(1)} %get-tuple-element.45, f32[2048]{0:T(1024)S(1)} %get-tuple-element.42, bf16[2048,256]{1,0:T(8,128)(2,1)S(1)} %collective-permute-done.6, ...), kind=kOutput, calls=%fused_computation.76 | convolution fusion | flops 958922752 | bytes 10438656 | tf_op jit(solution)/shard_map/dot_general | solution.py:50
  180.8 2.3 %collective-permute-start.8 = (bf16[512,128]{1,0:T(8,128)(2,1)S(1)}, bf16[512,128]{1,0:T(8,128)(2,1)}, u32[]{:S(2)}, u32[]{:S(2)}) collective-permute-start(bf16[512,128]{1,0:T(8,128)(2,1)S(1)} %get-tuple-element.24), channel_id=1, source_target_pairs={{0,50},{1,51},{2,0},{3,1},{4,54},{5,55},{6,4},{7,5},{8,58},{9,59},... | collective-permute-start | bytes 393224 | tf_op jit(solution)/shard_map/ppermute | solution.py:21
  183.4 3.6 %collective-permute-start.10 = (bf16[512,128]{1,0:T(8,128)(2,1)S(1)}, bf16[512,128]{1,0:T(8,128)(2,1)S(1)}, u32[]{:S(2)}, u32[]{:S(2)}) collective-permute-start(bf16[512,128]{1,0:T(8,128)(2,1)S(1)} %get-tuple-element.22), channel_id=1, source_target_pairs={{0,48},{1,49},{2,50},{3,51},{4,52},{5,53},{6,54},{7,55},{8,56},{9,... | collective-permute-start | bytes 393224 | tf_op jit(solution)/shard_map/ppermute | solution.py:21
  186.9 1.4 collective-permute-start.11
  188.3 3.1 %collective-permute-start.12 = (bf16[512,128]{1,0:T(8,128)(2,1)S(1)}, bf16[512,128]{1,0:T(8,128)(2,1)S(1)}, u32[]{:S(2)}, u32[]{:S(2)}) collective-permute-start(bf16[512,128]{1,0:T(8,128)(2,1)S(1)} %get-tuple-element.20), channel_id=1, source_target_pairs={{0,34},{1,35},{2,48},{3,49},{4,38},{5,39},{6,52},{7,53},{8,42},{9,... | collective-permute-start | bytes 393224 | tf_op jit(solution)/shard_map/ppermute | solution.py:21
  191.4 2.4 %collective-permute-start.13 = (bf16[512,128]{1,0:T(8,128)(2,1)S(1)}, bf16[512,128]{1,0:T(8,128)(2,1)S(1)}, u32[]{:S(2)}, u32[]{:S(2)}) collective-permute-start(bf16[512,128]{1,0:T(8,128)(2,1)S(1)} %get-tuple-element.19), channel_id=1, source_target_pairs={{0,32},{1,33},{2,34},{3,35},{4,36},{5,37},{6,38},{7,39},{8,40},{9,... | collective-permute-start | bytes 393224 | tf_op jit(solution)/shard_map/ppermute | solution.py:21
  193.8 3.1 %fusion.66 = f32[112,1792]{1,0:T(8,128)} fusion(bf16[112,1792]{1,0:T(8,128)(2,1)S(1)} %collective-permute-done.17, bf16[112,1792]{1,0:T(8,128)(2,1)S(1)} %collective-permute-done.18, bf16[112,1792]{1,0:T(8,128)(2,1)S(1)} %collective-permute-done.19, f32[448,1792]{1,0:T(8,128)} %get-tuple-element.49, s32[]{:T(128)S(6)} %select_n.699, ...), kind=kLoop, calls=%fused_computation.108 | loop fusion | flops 6021120 | bytes 2817476 | tf_op jit(solution)/shard_map/mul | solution.py:137
  196.9 9.5 %collective-permute-done.11 = bf16[512,128]{1,0:T(8,128)(2,1)S(1)} collective-permute-done((bf16[512,128]{1,0:T(8,128)(2,1)S(1)}, bf16[512,128]{1,0:T(8,128)(2,1)S(1)}, u32[]{:S(2)}, u32[]{:S(2)}) %collective-permute-start.11) | collective-permute-done | bytes 131104 | tf_op jit(solution)/shard_map/ppermute | solution.py:21
  206.4 4.4 %collective-permute-done.13 = bf16[512,128]{1,0:T(8,128)(2,1)S(1)} collective-permute-done((bf16[512,128]{1,0:T(8,128)(2,1)S(1)}, bf16[512,128]{1,0:T(8,128)(2,1)S(1)}, u32[]{:S(2)}, u32[]{:S(2)}) %collective-permute-start.13) | collective-permute-done | bytes 131104 | tf_op jit(solution)/shard_map/ppermute | solution.py:21
  210.8 2.6 %fusion.117 = f32[512,128]{1,0:T(8,128)} fusion(bf16[512,128]{1,0:T(8,128)(2,1)} %collective-permute-done.7, bf16[512,128]{1,0:T(8,128)(2,1)} %collective-permute-done.8, bf16[512,128]{1,0:T(8,128)(2,1)S(1)} %collective-permute-done.9, bf16[512,128]{1,0:T(8,128)(2,1)S(1)} %collective-permute-done.10, bf16[512,128]{1,0:T(8,128)(2,1)S(1)} %collective-permute-done.11, ...), kind=kLoop, calls=%fused_computation.178 | loop fusion | flops 4325376 | bytes 1444360 | tf_op jit(solution)/shard_map/mul | solution.py:160
  (57 shorter events, 6.6 us)
Async XLA Ops:
  0.6 11.5 %copy-start = (bf16[512,1792]{1,0:T(8,128)(2,1)S(1)}, bf16[512,1792]{1,0:T(8,128)(2,1)}, u32[]{:S(2)}) copy-start(bf16[512,1792]{1,0:T(8,128)(2,1)} %param.1) | copy-start | bytes 5505028
  3.7 104.7 %collective-permute-start.1 = (bf16[512,896]{1,0:T(8,128)(2,1)}, bf16[512,896]{1,0:T(8,128)(2,1)S(1)}, u32[]{:S(2)}, u32[]{:S(2)}) collective-permute-start(bf16[512,896]{1,0:T(8,128)(2,1)} %get-tuple-element.15), channel_id=1, source_target_pairs={{0,16},{1,48},{2,18},{3,50},{4,20},{5,52},{6,22},{7,54},{8,24},{9,... | collective-permute-start | bytes 2752520 | tf_op jit(solution)/shard_map/ppermute | solution.py:21
  9.4 108.7 %collective-permute-start = (bf16[512,896]{1,0:T(8,128)(2,1)}, bf16[512,896]{1,0:T(8,128)(2,1)}, u32[]{:S(2)}, u32[]{:S(2)}) collective-permute-start(bf16[512,896]{1,0:T(8,128)(2,1)} %get-tuple-element.14), channel_id=1, source_target_pairs={{0,0},{1,32},{2,2},{3,34},{4,4},{5,36},{6,6},{7,38},{8,8},{9,40},{... | collective-permute-start | bytes 2752520 | tf_op jit(solution)/shard_map/ppermute | solution.py:21
  15.7 114.6 %collective-permute-start.16 = (bf16[448,1792]{1,0:T(8,128)(2,1)}, bf16[448,1792]{1,0:T(8,128)(2,1)}, u32[]{:S(2)}, u32[]{:S(2)}) collective-permute-start(bf16[448,1792]{1,0:T(8,128)(2,1)} %multiply_convert_fusion.1), channel_id=1, source_target_pairs={{0,128},{1,129},{2,130},{3,131},{4,132},{5,133},{6,134},{7,135},{8... | collective-permute-start | bytes 4816904 | tf_op jit(solution)/shard_map/ppermute | solution.py:21
  21.2 109.2 %collective-permute-start.15 = (bf16[448,1792]{1,0:T(8,128)(2,1)}, bf16[448,1792]{1,0:T(8,128)(2,1)}, u32[]{:S(2)}, u32[]{:S(2)}) collective-permute-start(bf16[448,1792]{1,0:T(8,128)(2,1)} %multiply_convert_fusion.2), channel_id=1, source_target_pairs={{0,192},{1,193},{2,194},{3,195},{4,196},{5,197},{6,198},{7,199},{8... | collective-permute-start | bytes 4816904 | tf_op jit(solution)/shard_map/ppermute | solution.py:21
  24.9 105.5 %collective-permute-start.14 = (bf16[448,1792]{1,0:T(8,128)(2,1)}, bf16[448,1792]{1,0:T(8,128)(2,1)}, u32[]{:S(2)}, u32[]{:S(2)}) collective-permute-start(bf16[448,1792]{1,0:T(8,128)(2,1)} %multiply_convert_fusion.3), channel_id=1, source_target_pairs={{0,64},{1,65},{2,66},{3,67},{4,68},{5,69},{6,70},{7,71},{8,72},{9,... | collective-permute-start | bytes 4816904 | tf_op jit(solution)/shard_map/ppermute | solution.py:21
  108.4 11.9 %collective-permute-start.3 = (bf16[512,896]{1,0:T(8,128)(2,1)S(1)}, bf16[512,896]{1,0:T(8,128)(2,1)}, u32[]{:S(2)}, u32[]{:S(2)}) collective-permute-start(bf16[512,896]{1,0:T(8,128)(2,1)S(1)} %collective-permute-done.1), channel_id=1, source_target_pairs={{0,1},{1,0},{2,3},{3,2},{4,5},{5,4},{6,7},{7,6},{8,9},{9,8},{10,11... | collective-permute-start | bytes 2752520 | tf_op jit(solution)/shard_map/ppermute | solution.py:21
  118.1 3.8 %collective-permute-start.2 = (bf16[512,896]{1,0:T(8,128)(2,1)}, bf16[512,896]{1,0:T(8,128)(2,1)}, u32[]{:S(2)}, u32[]{:S(2)}) collective-permute-start(bf16[512,896]{1,0:T(8,128)(2,1)} %collective-permute-done), channel_id=1, source_target_pairs={{0,1},{1,0},{2,3},{3,2},{4,5},{5,4},{6,7},{7,6},{8,9},{9,8},{10,11... | collective-permute-start | bytes 2752520 | tf_op jit(solution)/shard_map/ppermute | solution.py:21
  125.7 26.0 %collective-permute-start.6 = (bf16[2048,256]{1,0:T(8,128)(2,1)S(1)}, bf16[2048,256]{1,0:T(8,128)(2,1)S(1)}, u32[]{:S(2)}, u32[]{:S(2)}) collective-permute-start(bf16[2048,256]{1,0:T(8,128)(2,1)S(1)} %multiply_convert_fusion.5), channel_id=1, source_target_pairs={{0,8},{1,9},{2,10},{3,11},{4,12},{5,13},{6,14},{7,15},{8,0},{9,1},... | collective-permute-start | bytes 3145736 | tf_op jit(solution)/shard_map/ppermute | solution.py:21
  127.3 45.0 %collective-permute-start.5 = (bf16[2048,256]{1,0:T(8,128)(2,1)S(1)}, bf16[2048,256]{1,0:T(8,128)(2,1)S(1)}, u32[]{:S(2)}, u32[]{:S(2)}) collective-permute-start(bf16[2048,256]{1,0:T(8,128)(2,1)S(1)} %multiply_convert_fusion.6), channel_id=1, source_target_pairs={{0,12},{1,13},{2,14},{3,15},{4,0},{5,1},{6,2},{7,3},{8,4},{9,5},{1... | collective-permute-start | bytes 3145736 | tf_op jit(solution)/shard_map/ppermute | solution.py:21
  130.3 44.5 %collective-permute-start.4 = (bf16[2048,256]{1,0:T(8,128)(2,1)S(1)}, bf16[2048,256]{1,0:T(8,128)(2,1)S(1)}, u32[]{:S(2)}, u32[]{:S(2)}) collective-permute-start(bf16[2048,256]{1,0:T(8,128)(2,1)S(1)} %multiply_convert_fusion.7), channel_id=1, source_target_pairs={{0,4},{1,5},{2,6},{3,7},{4,8},{5,9},{6,10},{7,11},{8,12},{9,13},{1... | collective-permute-start | bytes 3145736 | tf_op jit(solution)/shard_map/ppermute | solution.py:21
  140.6 42.7 %collective-permute-start.17 = (bf16[112,1792]{1,0:T(8,128)(2,1)S(1)}, bf16[112,1792]{1,0:T(8,128)(2,1)S(1)}, u32[]{:S(2)}, u32[]{:S(2)}) collective-permute-start(bf16[112,1792]{1,0:T(8,128)(2,1)S(1)} %get-tuple-element.18), channel_id=1, source_target_pairs={{0,16},{1,17},{2,18},{3,19},{4,20},{5,21},{6,22},{7,23},{8,24},{9,... | collective-permute-start | bytes 1204232 | tf_op jit(solution)/shard_map/ppermute | solution.py:21
  141.2 42.2 %collective-permute-start.18 = (bf16[112,1792]{1,0:T(8,128)(2,1)S(1)}, bf16[112,1792]{1,0:T(8,128)(2,1)S(1)}, u32[]{:S(2)}, u32[]{:S(2)}) collective-permute-start(bf16[112,1792]{1,0:T(8,128)(2,1)S(1)} %get-tuple-element.17), channel_id=1, source_target_pairs={{0,48},{1,49},{2,50},{3,51},{4,52},{5,53},{6,54},{7,55},{8,56},{9,... | collective-permute-start | bytes 1204232 | tf_op jit(solution)/shard_map/ppermute | solution.py:21
  151.7 35.3 %collective-permute-start.19 = (bf16[112,1792]{1,0:T(8,128)(2,1)S(1)}, bf16[112,1792]{1,0:T(8,128)(2,1)S(1)}, u32[]{:S(2)}, u32[]{:S(2)}) collective-permute-start(bf16[112,1792]{1,0:T(8,128)(2,1)S(1)} %get-tuple-element.16), channel_id=1, source_target_pairs={{0,32},{1,33},{2,34},{3,35},{4,36},{5,37},{6,38},{7,39},{8,40},{9,... | collective-permute-start | bytes 1204232 | tf_op jit(solution)/shard_map/ppermute | solution.py:21
  180.7 7.6 %collective-permute-start.7 = (bf16[512,128]{1,0:T(8,128)(2,1)S(1)}, bf16[512,128]{1,0:T(8,128)(2,1)}, u32[]{:S(2)}, u32[]{:S(2)}) collective-permute-start(bf16[512,128]{1,0:T(8,128)(2,1)S(1)} %get-tuple-element.25), channel_id=1, source_target_pairs={{0,2},{1,3},{2,16},{3,17},{4,6},{5,7},{6,20},{7,21},{8,10},{9,11},... | collective-permute-start | bytes 393224 | tf_op jit(solution)/shard_map/ppermute | solution.py:21
  180.8 10.6 %collective-permute-start.8 = (bf16[512,128]{1,0:T(8,128)(2,1)S(1)}, bf16[512,128]{1,0:T(8,128)(2,1)}, u32[]{:S(2)}, u32[]{:S(2)}) collective-permute-start(bf16[512,128]{1,0:T(8,128)(2,1)S(1)} %get-tuple-element.24), channel_id=1, source_target_pairs={{0,50},{1,51},{2,0},{3,1},{4,54},{5,55},{6,4},{7,5},{8,58},{9,59},... | collective-permute-start | bytes 393224 | tf_op jit(solution)/shard_map/ppermute | solution.py:21
  183.3 13.6 %collective-permute-start.9 = (bf16[512,128]{1,0:T(8,128)(2,1)S(1)}, bf16[512,128]{1,0:T(8,128)(2,1)S(1)}, u32[]{:S(2)}, u32[]{:S(2)}) collective-permute-start(bf16[512,128]{1,0:T(8,128)(2,1)S(1)} %get-tuple-element.23), channel_id=1, source_target_pairs={{0,16},{1,17},{2,18},{3,19},{4,20},{5,21},{6,22},{7,23},{8,24},{9,... | collective-permute-start | bytes 393224 | tf_op jit(solution)/shard_map/ppermute | solution.py:21
  183.4 13.6 %collective-permute-start.10 = (bf16[512,128]{1,0:T(8,128)(2,1)S(1)}, bf16[512,128]{1,0:T(8,128)(2,1)S(1)}, u32[]{:S(2)}, u32[]{:S(2)}) collective-permute-start(bf16[512,128]{1,0:T(8,128)(2,1)S(1)} %get-tuple-element.22), channel_id=1, source_target_pairs={{0,48},{1,49},{2,50},{3,51},{4,52},{5,53},{6,54},{7,55},{8,56},{9,... | collective-permute-start | bytes 393224 | tf_op jit(solution)/shard_map/ppermute | solution.py:21
  186.9 19.5 %collective-permute-start.11 = (bf16[512,128]{1,0:T(8,128)(2,1)S(1)}, bf16[512,128]{1,0:T(8,128)(2,1)S(1)}, u32[]{:S(2)}, u32[]{:S(2)}) collective-permute-start(bf16[512,128]{1,0:T(8,128)(2,1)S(1)} %get-tuple-element.21), channel_id=1, source_target_pairs={{0,18},{1,19},{2,32},{3,33},{4,22},{5,23},{6,36},{7,37},{8,26},{9,... | collective-permute-start | bytes 393224 | tf_op jit(solution)/shard_map/ppermute | solution.py:21
  188.3 18.1 %collective-permute-start.12 = (bf16[512,128]{1,0:T(8,128)(2,1)S(1)}, bf16[512,128]{1,0:T(8,128)(2,1)S(1)}, u32[]{:S(2)}, u32[]{:S(2)}) collective-permute-start(bf16[512,128]{1,0:T(8,128)(2,1)S(1)} %get-tuple-element.20), channel_id=1, source_target_pairs={{0,34},{1,35},{2,48},{3,49},{4,38},{5,39},{6,52},{7,53},{8,42},{9,... | collective-permute-start | bytes 393224 | tf_op jit(solution)/shard_map/ppermute | solution.py:21
  191.4 19.4 %collective-permute-start.13 = (bf16[512,128]{1,0:T(8,128)(2,1)S(1)}, bf16[512,128]{1,0:T(8,128)(2,1)S(1)}, u32[]{:S(2)}, u32[]{:S(2)}) collective-permute-start(bf16[512,128]{1,0:T(8,128)(2,1)S(1)} %get-tuple-element.19), channel_id=1, source_target_pairs={{0,32},{1,33},{2,34},{3,35},{4,36},{5,37},{6,38},{7,39},{8,40},{9,... | collective-permute-start | bytes 393224 | tf_op jit(solution)/shard_map/ppermute | solution.py:21

commit v2 on v0

v2 whole, which is shorter than its diff:
```python
import functools
import itertools

import jax
import jax.numpy as jnp
from jax import lax
from jax.experimental import pallas as pl
from jax.experimental.pallas import tpu as pltpu
from jax.sharding import PartitionSpec as P

F32, BF16 = jnp.float32, jnp.bfloat16

SIZES = (4, 4, 4, 2, 2)
PLACES = list(itertools.product(*(range(n) for n in SIZES)))
STEPS = (1, 3, 2)
Z_STEPS = (1, 7, 2, 6, 3, 5, 4)


def number(place):
    x, zh, y, zl, core = (p % n for p, n in zip(place, SIZES))
    return (4 * x + zh) * 16 + 4 * y + 2 * zl + core


def send(array, to):
    return lax.ppermute(array, ("row", "col"), [(number(p), number(to(*p))) for p in PLACES])


POWER = 13
LIFT = 120 / POWER
LOG_LIFT = LIFT * 0.6931471805599453


def split(norms):
    lead = norms.astype(BF16).astype(F32)
    trail = (norms - lead).astype(BF16).astype(F32)
    return lead, trail, lead + trail


def inverse(norms):
    return jnp.where(norms > 0, 1.0 / jnp.where(norms > 0, norms, 1.0), 0.0)


def raised(value, rows, cols):
    ratio = value * rows * (cols * 2.0**LIFT)
    p2 = ratio * ratio
    p4 = p2 * p2
    return p4 * p4 * (p4 * ratio)


def root(code, rows, cols):
    size = jnp.exp(jnp.log(jnp.abs(code)) * (1.0 / POWER) - LOG_LIFT)
    return jnp.where(code < 0, -size, size) * (rows * cols)


def upright(row):
    parts = [row[:, i : i + 128] for i in range(0, row.shape[1], 128)]
    return jnp.concatenate([jnp.broadcast_to(p, (128, 128)).T for p in parts], 0)


def dot(left, right, dim):
    return lax.dot_general(
        left, right, (((dim,), (dim,)), ((), ())), preferred_element_type=F32
    )


def run(body, outs, scratch, *args):
    smem, vmem = pl.BlockSpec(memory_space=pltpu.SMEM), pl.BlockSpec(memory_space=pltpu.VMEM)
    return pl.pallas_call(
        body,
        out_shape=[jax.ShapeDtypeStruct(shape, dtype) for shape, dtype in outs],
        in_specs=[smem] + [vmem] * (len(args) - 1),
        out_specs=[vmem] * len(outs),
        scratch_shapes=[pltpu.VMEM(shape, dtype) for shape, dtype in scratch],
        compiler_params=pltpu.CompilerParams(vmem_limit_bytes=48 * 1024 * 1024),
    )(*args)


BLOCK, CHUNK, TILES, WINDOW, IMAGE = 448, 112, 14, 1408, 512
PIECE = WINDOW + IMAGE


def first_tile(d):
    return 7 * (d // 2) + 3 * (d % 2)


def lead_in(d):
    return 64 * (d % 2)


def tile(i):
    return pl.ds(pl.multiple_of(i * 128, 128), 128)


def fill_window(g_ref, w_ref, d):
    for t in range(11):
        w_ref[:, t * 128 : (t + 1) * 128] = g_ref[:, tile(lax.rem(first_tile(d) + t, TILES))]


def block_rows(value, d):
    return jnp.where(d % 2 == 1, value[64:512], value[:448])


def column_norms(w_ref):
    return jnp.sqrt(jnp.sum(jnp.square(w_ref[...].astype(F32)), 0, keepdims=True))


def padded(rows, count):
    rows = jnp.concatenate(rows, 0)
    return jnp.concatenate([rows, jnp.zeros((count - rows.shape[0], rows.shape[1]), F32)], 0)


def right_first(step, at_ref, g_ref, out_ref, w_ref):
    d = lax.rem(at_ref[0] + step, 4)
    fill_window(g_ref, w_ref, d)
    lead, trail, norms = split(column_norms(w_ref))
    out_ref[BLOCK:, :] = padded([lead, trail], 16).astype(BF16)
    cols = inverse(norms)
    rows = block_rows(upright(cols[:, :512]), d)
    for t in range(11):
        lanes = slice(t * 128, (t + 1) * 128)
        part = block_rows(dot(w_ref[:, :512], w_ref[:, lanes], 0), d)
        out_ref[:BLOCK, lanes] = raised(part, rows, cols[:, lanes]).astype(BF16)


def right_second(at_ref, g_ref, in_1, in_3, in_2, out_1, out_3, out_2, own_ref, w_ref, e_ref, t_ref):
    d, zh = at_ref[0], at_ref[1]
    fill_window(g_ref, w_ref, d)
    own = column_norms(w_ref)
    squares, theirs = jnp.square(own), []
    for ref in (in_1, in_3, in_2):
        tail = ref[BLOCK:, :].astype(F32)
        norms = tail[0:1] + tail[1:2]
        squares += jnp.square(norms)
        theirs.append((ref, norms, block_rows(upright(norms[:, :512]), d)))
    lead, trail, norms = split(jnp.sqrt(squares))
    cols = inverse(norms)
    rows = block_rows(upright(cols[:, :512]), d)
    begin = pl.multiple_of(lead_in(d), 64)
    e_ref[:64, :] = jnp.zeros((64, WINDOW), F32)
    e_ref[BLOCK:, :] = jnp.zeros((64, WINDOW), F32)
    for t in range(11):
        lanes = slice(t * 128, (t + 1) * 128)
        part = block_rows(dot(w_ref[:, :512], w_ref[:, lanes], 0), d)
        for ref, their_cols, their_rows in theirs:
            part += root(ref[:BLOCK, lanes].astype(F32), their_rows, their_cols[:, lanes])
        e_ref[pl.ds(begin, BLOCK), lanes] = raised(part, rows, cols[:, lanes])
    for i in range(5):
        for j in range(4):
            t_ref[i * 128 : (i + 1) * 128, j * 128 : (j + 1) * 128] = e_ref[
                j * 128 : (j + 1) * 128, 384 + i * 128 : 512 + i * 128
            ].T
    blank = jnp.zeros((1, IMAGE), F32)
    tail = [jnp.concatenate([v, blank], 1) for v in (lead, trail, norms)]
    for step, ref in ((1, out_1), (3, out_3), (2, out_2), (0, own_ref)):
        chunk = lax.rem(zh + step, 4) * CHUNK
        piece = e_ref[pl.ds(pl.multiple_of(begin + chunk, 16), CHUNK), :]
        image = t_ref[pl.ds(pl.multiple_of(64 + begin + chunk, 16), CHUNK), :]
        ref[:CHUNK, :WINDOW] = piece.astype(ref.dtype)
        ref[:CHUNK, WINDOW:] = image.astype(ref.dtype)
        ref[CHUNK:, :] = padded(tail[:2] if step else tail[2:], 16).astype(ref.dtype)


def right_third(scale, at_ref, own_ref, in_1, in_3, in_2, out_ref, image_ref, r_ref):
    d, zh = at_ref[0], at_ref[1]
    begin = pl.multiple_of(lead_in(d) + zh * CHUNK, 16)
    for i, ref in enumerate((own_ref, in_1, in_3, in_2)):
        tail = ref[CHUNK:, :].astype(F32)
        norms = (tail[0:1] if i == 0 else tail[0:1] + tail[1:2])[:, :WINDOW]
        r_ref[...] = upright(norms[:, :1024])
        rows = r_ref[pl.ds(begin, CHUNK), :]
        image_rows = r_ref[pl.ds(pl.multiple_of(448 + begin, 16), CHUNK), :]
        for t in range(15):
            lanes = slice(t * 128, (t + 1) * 128)
            code = ref[:CHUNK, lanes].astype(F32)
            if t < 11:
                to, here, part = out_ref, lanes, root(code, rows, norms[:, lanes])
            else:
                here = slice((t - 11) * 128, (t - 10) * 128)
                to, part = image_ref, root(code, image_rows, norms[:, here])
            if i == 0:
                to[:, here] = part * scale
            else:
                to[:, here] += part * scale


def right_last(at_ref, base_ref, image_ref, out_ref):
    d = at_ref[0]
    for t in range(11):
        out_ref[:, tile(lax.rem(first_tile(d) + t, TILES))] = base_ref[:, t * 128 : (t + 1) * 128]
    even = d % 2 == 0
    for t in range(3):
        part = jnp.where(
            even, image_ref[:, (t + 1) * 128 : (t + 2) * 128], image_ref[:, t * 128 : (t + 1) * 128]
        )
        out_ref[:, tile(lax.rem(first_tile(d) + 11 + t, TILES))] = part


SUB, BASE, ROWS = 128, 1024, 1152


def sub(i):
    return pl.ds(pl.multiple_of(i * SUB, SUB), SUB)


def base_subs(core, b):
    return [4 * a + (core ^ (a > b).astype(jnp.int32)) + 2 * h for a in range(4) for h in (0, 1)]


def more_sub(core, b, zl):
    return 4 * b + lax.rem(2 * zl + core + 1, 4)


def two_cols(ref, core, b):
    return jnp.concatenate([ref[pl.ds(4 * b + core + 2 * zl, 1), :] for zl in (0, 1)], 1)


def left_first(at_ref, far, near, far_2, near_2, out_1, out_3, out_2, own_ref, norm_ref, a_ref, b_ref, i_ref, s_ref):
    zh, y, core = at_ref[1], at_ref[2], at_ref[4]
    for p, ref in enumerate((far, near, far_2, near_2)):
        j = 2 * ((p // 2) ^ core) + lax.rem(p + zh, 2)
        a_ref[pl.ds(pl.multiple_of(j * 512, 512), 512), :] = ref[...]
    leads, trails, lanes = [], [], []
    for i in range(16):
        rows = slice(i * SUB, (i + 1) * SUB)
        squares = jnp.sum(jnp.square(a_ref[rows, :].astype(F32)), 1, keepdims=True)
        row = jnp.broadcast_to(jnp.sqrt(squares), (SUB, SUB)).T[0:1]
        lead, trail, norms = split(row)
        leads.append(lead), trails.append(trail), lanes.append(norms)
        i_ref[rows, :] = upright(inverse(norms))
    tail = jnp.concatenate([jnp.concatenate(leads, 0), jnp.concatenate(trails, 0)], 1).astype(BF16)
    norm_ref[...] = jnp.concatenate(lanes, 0)
    s_ref[...] = inverse(norm_ref[...])
    for step, out in ((1, out_1), (3, out_3), (2, out_2), (0, own_ref)):
        b = lax.rem(y + step, 4)
        for zl in (0, 1):
            b_ref[zl * SUB : (zl + 1) * SUB, :] = a_ref[sub(4 * b + core + 2 * zl), :]
        cols = two_cols(s_ref, core, b)
        for k, i in enumerate(base_subs(core, b)):
            part = dot(a_ref[sub(i), :], b_ref[...], 1)
            if step:
                scale = i_ref[sub(i), :]
                part = raised(part, jnp.concatenate([scale, scale], 1), cols).astype(BF16)
            out[k * SUB : (k + 1) * SUB, :] = part
        for zl in (0, 1):
            here = slice(zl * SUB, (zl + 1) * SUB)
            i = more_sub(core, b, zl)
            part = dot(a_ref[sub(i), :], b_ref[here, :], 1)
            if step:
                part = raised(part, i_ref[sub(i), :], cols[:, here]).astype(BF16)
            out[BASE:ROWS, here] = part
        if step:
            out[ROWS:, :] = tail


def left_second(at_ref, own_ref, norm_ref, in_1, in_3, in_2, *refs):
    outs, (e_ref, s_ref, lead_ref, trail_ref, n_ref) = refs[:8], refs[8:]
    zh, y, zl, core = (at_ref[i] for i in (1, 2, 3, 4))
    squares = jnp.square(norm_ref[...])
    for k, ref in enumerate((in_1, in_3, in_2)):
        tail = ref[ROWS:, :].astype(F32)
        norms = tail[:, :SUB] + tail[:, SUB:]
        squares += jnp.square(norms)
        s_ref[k] = norms
    lead_ref[...], trail_ref[...], n_ref[...] = split(jnp.sqrt(squares))
    s_ref[3] = inverse(n_ref[...])
    sources = [(ref, k) for k, ref in enumerate((in_1, in_3, in_2))]
    cols = [two_cols(s_ref.at[k], core, y) for k in range(4)]
    r = lambda k, i: upright(s_ref.at[k][pl.ds(i, 1), :])
    for j, i in enumerate(base_subs(core, y)):
        rows = slice(j * SUB, (j + 1) * SUB)
        part = own_ref[rows, :]
        for ref, k in sources:
            scale = r(k, i)
            part += root(ref[rows, :].astype(F32), jnp.concatenate([scale, scale], 1), cols[k])
        scale = r(3, i)
        e_ref[rows, :] = raised(part, jnp.concatenate([scale, scale], 1), cols[3])
    for l in (0, 1):
        here = slice(l * SUB, (l + 1) * SUB)
        i = more_sub(core, y, l)
        part = own_ref[BASE:ROWS, here]
        for ref, k in sources:
            part += root(ref[BASE:ROWS, here].astype(F32), r(k, i), cols[k][:, here])
        e_ref[BASE:ROWS, here] = raised(part, r(3, i), cols[3][:, here])
    for step, out in zip((*Z_STEPS, 0), outs):
        z = lax.rem(2 * zh + zl + step, 8)
        to_h, to_l = z // 2, lax.rem(z, 2)
        lanes = tile(to_l)
        out[:256, :] = e_ref[pl.ds(pl.multiple_of(to_h * 256, 256), 256), lanes].astype(out.dtype)
        out[256:384, :] = e_ref[BASE:ROWS, lanes].astype(out.dtype)
        first = 4 * to_h + (core ^ (to_h > y).astype(jnp.int32))
        picks = [first, first + 2, more_sub(core, y, to_l), 4 * y + 2 * to_l + core]
        tail = [ref[pl.ds(i, 1), :] for ref in ((lead_ref, trail_ref) if step else (n_ref,)) for i in picks]
        out[384:, :] = padded(tail, 16).astype(out.dtype)


def left_third(scale, at_ref, *refs):
    sources, (base_ref, more_ref, same_ref, other_ref, sum_ref) = refs[:8], refs[8:]
    zh, y, zl = at_ref[1], at_ref[2], at_ref[3]
    for k, ref in enumerate(sources):
        tail = ref[384:, :].astype(F32)
        norms = tail[0:4] if k == 0 else tail[0:4] + tail[4:8]
        for j in range(3):
            rows = slice(j * SUB, (j + 1) * SUB)
            part = root(ref[rows, :].astype(F32), upright(norms[j : j + 1]), norms[3:4]) * scale
            if k == 0:
                sum_ref[rows, :] = part
            else:
                sum_ref[rows, :] += part
    first, second, more = (sum_ref[j * SUB : (j + 1) * SUB, :] for j in range(3))
    base_ref[...] = sum_ref[:256, :]
    more_ref[...] = more
    same_ref[...] = jnp.where(zh == y, more, jnp.where(zl == 0, first, second)).T
    other_ref[...] = jnp.where(zl == 0, second, first).T


def left_last(at_ref, base_ref, more_ref, same_ref, other_ref, out_ref):
    zh, y, zl, core = (at_ref[i] for i in (1, 2, 3, 4))
    n, parity, diagonal = 2 * zl + core, core ^ (zh > y).astype(jnp.int32), zh == y
    out_ref[sub(parity), :] = base_ref[:SUB, :]
    out_ref[sub(parity + 2), :] = base_ref[SUB:, :]
    out_ref[sub(jnp.where(diagonal, lax.rem(n + 3, 4), 2 * zl + 1 - parity)), :] = same_ref[...]
    out_ref[sub(jnp.where(diagonal, lax.rem(n + 1, 4), 2 * (1 - zl) + 1 - parity)), :] = jnp.where(
        diagonal, more_ref[...], other_ref[...]
    )


def mirror(step):
    def to(x, zh, y, zl, core):
        if zh != y:
            return (x, y, zh, zl ^ step, core ^ (zh > y))
        n = (2 * zl + core + 1 - step) % 4
        return (x, zh, y, n // 2, n % 2)

    return to


def along_z(step):
    def to(x, zh, y, zl, core):
        z = (2 * zh + zl + step) % 8
        return (x, z // 2, y, z % 2, core)

    return to


def shards(gradient):
    rows, width = gradient.shape
    row, col = lax.axis_index("row"), lax.axis_index("col")
    x, zh, y, zl, core = row // 4, row % 4, col // 4, col // 2 % 2, col % 2
    at = jnp.stack([x, zh, y, zl, core, x, x, x]).astype(jnp.int32)
    barrier = lax.optimization_barrier
    half = width // 2

    cut = lambda parity: lax.dynamic_slice_in_dim(gradient, parity * half, half, 1)
    near, far = cut((zh + 1) % 2), cut(zh % 2)
    near = send(near, lambda x, zh, y, zl, core: (x, 2 * core + (zh + 1) % 2, y, zl, zh // 2))
    first = lambda s: run(
        functools.partial(right_first, s),
        [((BLOCK + 16, WINDOW), BF16)],
        [((rows, WINDOW), BF16)],
        at,
        gradient,
    )[0]
    over_x = lambda s, v: send(v, lambda x, zh, y, zl, core: (x + s, zh, y, zl, core))
    right_2 = over_x(2, first(2))
    code_1, code_3 = first(1), first(3)
    near, far, right_2, code_1, code_3 = barrier((near, far, right_2, code_1, code_3))
    far = send(far, lambda x, zh, y, zl, core: (x, 2 * core + zh % 2, y, zl, zh // 2))
    right_1, right_3 = over_x(1, code_1), over_x(3, code_3)
    near, far, right_1, right_2, right_3 = barrier((near, far, right_1, right_2, right_3))

    swap = lambda x, zh, y, zl, core: (x, zh, y, zl, 1 - core)
    far_2, near_2 = send(far, swap), send(near, swap)
    piece = (CHUNK + 16, PIECE)
    code_1, code_3, code_2, right_own = run(
        right_second,
        [(piece, BF16)] * 3 + [(piece, F32)],
        [((rows, WINDOW), BF16), ((512, WINDOW), F32), ((640, IMAGE), F32)],
        at,
        gradient,
        right_1,
        right_3,
        right_2,
    )
    over_z = lambda s, v: send(v, lambda x, zh, y, zl, core: (x, zh + s, y, zl, core))
    right_1, right_3 = over_z(1, code_1), over_z(3, code_3)

    far, near, far_2, near_2, code_2 = barrier((far, near, far_2, near_2, code_2))
    packed = (ROWS + 16, 256)
    left_1, left_3, left_2, left_own, norms = run(
        left_first,
        [(packed, BF16)] * 3 + [((ROWS, 256), F32), ((16, SUB), F32)],
        [((2048, half), BF16), ((256, half), BF16), ((2048, SUB), F32), ((16, SUB), F32)],
        at,
        far,
        near,
        far_2,
        near_2,
    )
    over_y = lambda s, v: send(v, lambda x, zh, y, zl, core: (x, zh, y + s, zl, core))
    left_1, left_3 = over_y(1, left_1), over_y(3, left_3)
    left_1, left_3, left_2, right_1, right_3, code_2 = barrier((left_1, left_3, left_2, right_1, right_3, code_2))
    left_2, right_2 = over_y(2, left_2), over_z(2, code_2)

    piece = (400, SUB)
    codes = run(
        left_second,
        [(piece, BF16)] * 7 + [(piece, F32)],
        [((ROWS, 256), F32), ((4, 16, SUB), F32)] + [((16, SUB), F32)] * 3,
        at,
        left_own,
        norms,
        left_1,
        left_3,
        left_2,
    )
    right_2, codes = barrier((right_2, codes))
    arrived = [send(code, along_z(s)) for s, code in zip(Z_STEPS, codes)]

    right_base, image = run(
        functools.partial(right_third, 1.0 / (rows * 16)),
        [((CHUNK, WINDOW), F32), ((CHUNK, IMAGE), F32)],
        [((1024, 128), F32)],
        at,
        right_own,
        right_1,
        right_3,
        right_2,
    )
    image = over_x(1, image)
    right_gram = run(right_last, [((CHUNK, width), F32)], [], at, right_base, image)[0]

    square = ((SUB, SUB), F32)
    base, more, same, other = run(
        functools.partial(left_third, 1.0 / (width * 16)),
        [((256, SUB), F32), square, square, square],
        [((384, SUB), F32)],
        at,
        codes[7],
        *arrived,
    )
    same, other = send(same, mirror(0)), send(other, mirror(1))
    left_gram = run(left_last, [((512, SUB), F32)], [], at, base, more, same, other)[0]
    return (left_gram, right_gram)


def solution(mesh):
    in_specs = (P("row", "col"),)
    out_specs = (P("row", "col"), P(("col", "row"), None))
    return jax.shard_map(shards, mesh=mesh, in_specs=in_specs, out_specs=out_specs, check_vma=False)
```

time: 535 us -> 204 us (0.38)
  the two profiles are of different devices: /device:TPU:25 before, /device:TPU:48 now
where the time goes in v2:
time: 204 us; the launch traced here: 200 us
  waiting for transfers between devices  99.7 us (49%)
  starting transfers between devices  62.2 us (30%)
  Pallas kernels  34 us (17%)
  local copies, waits for them, and re-layouts  3.11 us (2%)
    ppermute x23, waiting for transfers between devices, send(): lax.ppermute(array, ('row', 'col'), [(number(p), number(to(*p))) for p in...  99.7 us
    ppermute x23, starting transfers between devices, send(): lax.ppermute(array, ('row', 'col'), [(number(p), number(to(*p))) for p in...  62.2 us
    pallas_call x10, Pallas kernels, run(): pl.pallas_call(body, out_shape=[jax.ShapeDtypeStruct(shape, dtype) for sh...  34 us
  transfers between devices with their start and end apart: 23, of which 10 were waited for; matrix products, arithmetic and copies ran while one was open for 0% of the time, Pallas kernels for 11%

profile of v2, /device:TPU:48, one launch (start us, length us, event | category | flops | bytes accessed | tf_op | source)
XLA Modules:
  0.0 199.9 jit_solution(11953646438234049498)
XLA Ops:
  2.3 3.1 %shard_map.30 = bf16[464,1408]{1,0:T(8,128)(2,1)S(1)} custom-call(s32[8]{0:T(128)S(1)} %stack.26.at_ref, bf16[512,1792]{1,0:T(8,128)(2,1)S(1)} %copy-done), custom_call_target="tpu_custom_call" | custom-call | tf_op jit(solution)/shard_map/pallas_call | solution.py:68
  5.4 3.1 %collective-permute-start.1 = (bf16[464,1408]{1,0:T(8,128)(2,1)S(1)}, bf16[464,1408]{1,0:T(8,128)(2,1)}, u32[]{:S(2)}, u32[]{:S(2)}) collective-permute-start(bf16[464,1408]{1,0:T(8,128)(2,1)S(1)} %shard_map.30), channel_id=1, source_target_pairs={{0,128},{1,129},{2,130},{3,131},{4,132},{5,133},{6,134},{7,135},{8... | collective-permute-start | bytes 3919880 | tf_op jit(solution)/shard_map/ppermute | solution.py:25
  8.8 3.3 %collective-permute-start = (bf16[512,896]{1,0:T(8,128)(2,1)S(1)}, bf16[512,896]{1,0:T(8,128)(2,1)S(1)}, u32[]{:S(2)}, u32[]{:S(2)}) collective-permute-start(bf16[512,896]{1,0:T(8,128)(2,1)S(1)} %get-tuple-element.109), channel_id=1, source_target_pairs={{0,16},{1,48},{2,18},{3,50},{4,20},{5,52},{6,22},{7,54},{8,24},{9,... | collective-permute-start | bytes 2752520 | tf_op jit(solution)/shard_map/ppermute | solution.py:25
  12.0 3.1 %shard_map.31 = bf16[464,1408]{1,0:T(8,128)(2,1)S(1)} custom-call(s32[8]{0:T(128)S(1)} %stack.26.at_ref, bf16[512,1792]{1,0:T(8,128)(2,1)S(1)} %copy-done.1), custom_call_target="tpu_custom_call" | custom-call | tf_op jit(solution)/shard_map/pallas_call | solution.py:68
  15.2 3.1 %shard_map.32 = bf16[464,1408]{1,0:T(8,128)(2,1)S(1)} custom-call(s32[8]{0:T(128)S(1)} %stack.26.at_ref, bf16[512,1792]{1,0:T(8,128)(2,1)S(1)} %copy-done.1), custom_call_target="tpu_custom_call" | custom-call | tf_op jit(solution)/shard_map/pallas_call | solution.py:68
  18.3 14.0 %collective-permute-done.near = bf16[512,896]{1,0:T(8,128)(2,1)S(1)} collective-permute-done((bf16[512,896]{1,0:T(8,128)(2,1)S(1)}, bf16[512,896]{1,0:T(8,128)(2,1)S(1)}, u32[]{:S(2)}, u32[]{:S(2)}) %collective-permute-start) | collective-permute-done | bytes 917536 | tf_op jit(solution)/shard_map/ppermute | solution.py:25
  32.3 5.2 %collective-permute-done.1.in_2 = bf16[464,1408]{1,0:T(8,128)(2,1)} collective-permute-done((bf16[464,1408]{1,0:T(8,128)(2,1)S(1)}, bf16[464,1408]{1,0:T(8,128)(2,1)}, u32[]{:S(2)}, u32[]{:S(2)}) %collective-permute-start.1) | collective-permute-done | bytes 1306656 | tf_op jit(solution)/shard_map/ppermute | solution.py:25
  39.0 1.7 collective-permute-start.4
  41.5 26.8 %collective-permute-done.3.in_1 = bf16[464,1408]{1,0:T(8,128)(2,1)S(1)} collective-permute-done((bf16[464,1408]{1,0:T(8,128)(2,1)S(1)}, bf16[464,1408]{1,0:T(8,128)(2,1)S(1)}, u32[]{:S(2)}, u32[]{:S(2)}) %collective-permute-start.3) | collective-permute-done | bytes 1306656 | tf_op jit(solution)/shard_map/ppermute | solution.py:25
  68.3 1.8 collective-permute-start.5
  70.4 7.3 %shard_map.33 = (bf16[128,1920]{1,0:T(8,128)(2,1)S(1)}, bf16[128,1920]{1,0:T(8,128)(2,1)S(1)}, bf16[128,1920]{1,0:T(8,128)(2,1)S(1)}, f32[128,1920]{1,0:T(8,128)S(1)}) custom-call(s32[8]{0:T(128)S(1)} %stack.26.at_ref, bf16[512,1792]{1,0:T(8,128)(2,1)} %g_ref.7, bf16[464,1408]{1,0:T(8,128)(2,1)S(1)} %collective-permute-done.3.in_1, ...), custom_call_target="tpu_custom_call" | custom-call | tf_op jit(solution)/shard_map/pallas_call | solution.py:68
  77.8 7.7 %shard_map.34 = (bf16[1168,256]{1,0:T(8,128)(2,1)S(1)}, bf16[1168,256]{1,0:T(8,128)(2,1)S(1)}, bf16[1168,256]{1,0:T(8,128)(2,1)S(1)}, f32[1152,256]{1,0:T(8,128)}, f32[16,128]{1,0:T(8,128)S(1)}) custom-call(s32[8]{0:T(128)S(1)} %stack.26.at_ref, bf16[512,896]{1,0:T(8,128)(2,1)S(1)} %collective-permute-done.2.far, ...), custom_call_target="tpu_custom_call" | custom-call | tf_op jit(solution)/shard_map/pallas_call | solution.py:68
  87.6 11.4 %collective-permute-start.9 = (bf16[128,1920]{1,0:T(8,128)(2,1)S(1)}, bf16[128,1920]{1,0:T(8,128)(2,1)S(1)}, u32[]{:S(2)}, u32[]{:S(2)}) collective-permute-start(bf16[128,1920]{1,0:T(8,128)(2,1)S(1)} %get-tuple-element.73), channel_id=1, source_target_pairs={{0,16},{1,17},{2,18},{3,19},{4,20},{5,21},{6,22},{7,23},{8,24},{9,... | collective-permute-start | bytes 1474568 | tf_op jit(solution)/shard_map/ppermute | solution.py:25
  99.0 2.3 %collective-permute-start.10 = (bf16[128,1920]{1,0:T(8,128)(2,1)S(1)}, bf16[128,1920]{1,0:T(8,128)(2,1)S(1)}, u32[]{:S(2)}, u32[]{:S(2)}) collective-permute-start(bf16[128,1920]{1,0:T(8,128)(2,1)S(1)} %get-tuple-element.74), channel_id=1, source_target_pairs={{0,48},{1,49},{2,50},{3,51},{4,52},{5,53},{6,54},{7,55},{8,56},{9,... | collective-permute-start | bytes 1474568 | tf_op jit(solution)/shard_map/ppermute | solution.py:25
  101.3 19.5 %collective-permute-done.9.in_1 = bf16[128,1920]{1,0:T(8,128)(2,1)S(1)} collective-permute-done((bf16[128,1920]{1,0:T(8,128)(2,1)S(1)}, bf16[128,1920]{1,0:T(8,128)(2,1)S(1)}, u32[]{:S(2)}, u32[]{:S(2)}) %collective-permute-start.9) | collective-permute-done | bytes 491552 | tf_op jit(solution)/shard_map/ppermute | solution.py:25
  120.8 3.9 %collective-permute-done.10.in_3 = bf16[128,1920]{1,0:T(8,128)(2,1)S(1)} collective-permute-done((bf16[128,1920]{1,0:T(8,128)(2,1)S(1)}, bf16[128,1920]{1,0:T(8,128)(2,1)S(1)}, u32[]{:S(2)}, u32[]{:S(2)}) %collective-permute-start.10) | collective-permute-done | bytes 491552 | tf_op jit(solution)/shard_map/ppermute | solution.py:25
  126.4 3.1 %collective-permute-start.11 = (bf16[128,1920]{1,0:T(8,128)(2,1)S(1)}, bf16[128,1920]{1,0:T(8,128)(2,1)S(1)}, u32[]{:S(2)}, u32[]{:S(2)}) collective-permute-start(bf16[128,1920]{1,0:T(8,128)(2,1)S(1)} %get-tuple-element.76), channel_id=1, source_target_pairs={{0,32},{1,33},{2,34},{3,35},{4,36},{5,37},{6,38},{7,39},{8,40},{9,... | collective-permute-start | bytes 1474568 | tf_op jit(solution)/shard_map/ppermute | solution.py:25
  129.4 10.9 %collective-permute-done.12.in_2 = bf16[1168,256]{1,0:T(8,128)(2,1)S(1)} collective-permute-done((bf16[1168,256]{1,0:T(8,128)(2,1)S(1)}, bf16[1168,256]{1,0:T(8,128)(2,1)S(1)}, u32[]{:S(2)}, u32[]{:S(2)}) %collective-permute-start.12) | collective-permute-done | bytes 598048 | tf_op jit(solution)/shard_map/ppermute | solution.py:25
  141.6 2.7 %shard_map.35 = (bf16[400,128]{1,0:T(8,128)(2,1)S(1)}, bf16[400,128]{1,0:T(8,128)(2,1)S(1)}, bf16[400,128]{1,0:T(8,128)(2,1)S(1)}, bf16[400,128]{1,0:T(8,128)(2,...) custom-call(s32[8]{0:T(128)S(1)} %stack.26.at_ref, ...), custom_call_target="tpu_custom_call" | custom-call | tf_op jit(solution)/shard_map/pallas_call | solution.py:68
  144.4 8.4 %collective-permute-start.14 = (bf16[400,128]{1,0:T(8,128)(2,1)S(1)}, bf16[400,128]{1,0:T(8,128)(2,1)S(1)}, u32[]{:S(2)}, u32[]{:S(2)}) collective-permute-start(bf16[400,128]{1,0:T(8,128)(2,1)S(1)} %get-tuple-element.92), channel_id=1, source_target_pairs={{0,50},{1,51},{2,0},{3,1},{4,54},{5,55},{6,4},{7,5},{8,58},{9,59},... | collective-permute-start | bytes 307208 | tf_op jit(solution)/shard_map/ppermute | solution.py:25
  152.7 5.2 %collective-permute-start.15 = (bf16[400,128]{1,0:T(8,128)(2,1)S(1)}, bf16[400,128]{1,0:T(8,128)(2,1)S(1)}, u32[]{:S(2)}, u32[]{:S(2)}) collective-permute-start(bf16[400,128]{1,0:T(8,128)(2,1)S(1)} %get-tuple-element.93), channel_id=1, source_target_pairs={{0,16},{1,17},{2,18},{3,19},{4,20},{5,21},{6,22},{7,23},{8,24},{9,... | collective-permute-start | bytes 307208 | tf_op jit(solution)/shard_map/ppermute | solution.py:25
  158.0 2.6 %shard_map.38 = (f32[112,1408]{1,0:T(8,128)S(1)}, f32[112,512]{1,0:T(8,128)S(1)}) custom-call(s32[8]{0:T(128)S(1)} %stack.26.at_ref, f32[128,1920]{1,0:T(8,128)S(1)} %get-tuple-element.102.own_ref, bf16[128,1920]{1,0:T(8,128)(2,1)S(1)} %collective-permute-done.9.in_1, bf16[128,1920]{1,0:T(8,128)(2,1)S(1)} %collective-permute-done.10.in_3, ...), custom_call_target="tpu_custom_call" | custom-call | tf_op jit(solution)/shard_map/pallas_call | solution.py:68
  160.7 1.7 collective-permute-start.16
  162.4 3.1 %collective-permute-start.17 = (bf16[400,128]{1,0:T(8,128)(2,1)S(1)}, bf16[400,128]{1,0:T(8,128)(2,1)S(1)}, u32[]{:S(2)}, u32[]{:S(2)}) collective-permute-start(bf16[400,128]{1,0:T(8,128)(2,1)S(1)} %get-tuple-element.95), channel_id=1, source_target_pairs={{0,18},{1,19},{2,32},{3,33},{4,22},{5,23},{6,36},{7,37},{8,26},{9,... | collective-permute-start | bytes 307208 | tf_op jit(solution)/shard_map/ppermute | solution.py:25
  165.6 1.9 collective-permute-start.18
  167.5 2.4 %collective-permute-start.19 = (bf16[400,128]{1,0:T(8,128)(2,1)S(1)}, bf16[400,128]{1,0:T(8,128)(2,1)S(1)}, u32[]{:S(2)}, u32[]{:S(2)}) collective-permute-start(bf16[400,128]{1,0:T(8,128)(2,1)S(1)} %get-tuple-element.97), channel_id=1, source_target_pairs={{0,32},{1,33},{2,34},{3,35},{4,36},{5,37},{6,38},{7,39},{8,40},{9,... | collective-permute-start | bytes 307208 | tf_op jit(solution)/shard_map/ppermute | solution.py:25
  169.9 4.4 %collective-permute-done.17.refs_5_ = bf16[400,128]{1,0:T(8,128)(2,1)S(1)} collective-permute-done((bf16[400,128]{1,0:T(8,128)(2,1)S(1)}, bf16[400,128]{1,0:T(8,128)(2,1)S(1)}, u32[]{:S(2)}, u32[]{:S(2)}) %collective-permute-start.17) | collective-permute-done | bytes 102432 | tf_op jit(solution)/shard_map/ppermute | solution.py:25
  174.3 5.7 %collective-permute-done.18.refs_6_ = bf16[400,128]{1,0:T(8,128)(2,1)S(1)} collective-permute-done((bf16[400,128]{1,0:T(8,128)(2,1)S(1)}, bf16[400,128]{1,0:T(8,128)(2,1)S(1)}, u32[]{:S(2)}, u32[]{:S(2)}) %collective-permute-start.18) | collective-permute-done | bytes 102432 | tf_op jit(solution)/shard_map/ppermute | solution.py:25
  181.5 4.5 %collective-permute-start.20 = (f32[128,128]{1,0:T(8,128)S(1)}, f32[128,128]{1,0:T(8,128)S(1)}, u32[]{:S(2)}, u32[]{:S(2)}) collective-permute-start(f32[128,128]{1,0:T(8,128)S(1)} %get-tuple-element.100), channel_id=1, source_target_pairs={{0,1},{1,2},{2,3},{3,0},{4,16},{5,17},{6,18},{7,19},{8,32},{9,33},... | collective-permute-start | bytes 196616 | tf_op jit(solution)/shard_map/ppermute | solution.py:25
  186.0 1.9 collective-permute-start.21
  187.9 3.8 %collective-permute-done.20.same_ref = f32[128,128]{1,0:T(8,128)S(1)} collective-permute-done((f32[128,128]{1,0:T(8,128)S(1)}, f32[128,128]{1,0:T(8,128)S(1)}, u32[]{:S(2)}, u32[]{:S(2)}) %collective-permute-start.20) | collective-permute-done | bytes 65568 | tf_op jit(solution)/shard_map/ppermute | solution.py:25
  191.7 5.2 %collective-permute-done.21.other_ref = f32[128,128]{1,0:T(8,128)S(1)} collective-permute-done((f32[128,128]{1,0:T(8,128)S(1)}, f32[128,128]{1,0:T(8,128)S(1)}, u32[]{:S(2)}, u32[]{:S(2)}) %collective-permute-start.21) | collective-permute-done | bytes 65568 | tf_op jit(solution)/shard_map/ppermute | solution.py:25
  (32 shorter events, 13.8 us)
Async XLA Ops:
  0.8 1.5 copy-start
  2.3 6.3 %copy-start.1 = (bf16[512,1792]{1,0:T(8,128)(2,1)S(1)}, bf16[512,1792]{1,0:T(8,128)(2,1)}, u32[]{:S(2)}) copy-start(bf16[512,1792]{1,0:T(8,128)(2,1)} %g_ref.7) | copy-start | bytes 5505028
  5.4 32.1 %collective-permute-start.1 = (bf16[464,1408]{1,0:T(8,128)(2,1)S(1)}, bf16[464,1408]{1,0:T(8,128)(2,1)}, u32[]{:S(2)}, u32[]{:S(2)}) collective-permute-start(bf16[464,1408]{1,0:T(8,128)(2,1)S(1)} %shard_map.30), channel_id=1, source_target_pairs={{0,128},{1,129},{2,130},{3,131},{4,132},{5,133},{6,134},{7,135},{8... | collective-permute-start | bytes 3919880 | tf_op jit(solution)/shard_map/ppermute | solution.py:25
  8.8 23.5 %collective-permute-start = (bf16[512,896]{1,0:T(8,128)(2,1)S(1)}, bf16[512,896]{1,0:T(8,128)(2,1)S(1)}, u32[]{:S(2)}, u32[]{:S(2)}) collective-permute-start(bf16[512,896]{1,0:T(8,128)(2,1)S(1)} %get-tuple-element.109), channel_id=1, source_target_pairs={{0,16},{1,48},{2,18},{3,50},{4,20},{5,52},{6,22},{7,54},{8,24},{9,... | collective-permute-start | bytes 2752520 | tf_op jit(solution)/shard_map/ppermute | solution.py:25
  37.5 30.8 %collective-permute-start.3 = (bf16[464,1408]{1,0:T(8,128)(2,1)S(1)}, bf16[464,1408]{1,0:T(8,128)(2,1)S(1)}, u32[]{:S(2)}, u32[]{:S(2)}) collective-permute-start(bf16[464,1408]{1,0:T(8,128)(2,1)S(1)} %shard_map.31), channel_id=1, source_target_pairs={{0,64},{1,65},{2,66},{3,67},{4,68},{5,69},{6,70},{7,71},{8,72},{9,... | collective-permute-start | bytes 3919880 | tf_op jit(solution)/shard_map/ppermute | solution.py:25
  39.0 29.3 %collective-permute-start.4 = (bf16[464,1408]{1,0:T(8,128)(2,1)S(1)}, bf16[464,1408]{1,0:T(8,128)(2,1)S(1)}, u32[]{:S(2)}, u32[]{:S(2)}) collective-permute-start(bf16[464,1408]{1,0:T(8,128)(2,1)S(1)} %shard_map.32), channel_id=1, source_target_pairs={{0,192},{1,193},{2,194},{3,195},{4,196},{5,197},{6,198},{7,199},{8... | collective-permute-start | bytes 3919880 | tf_op jit(solution)/shard_map/ppermute | solution.py:25
  40.8 0.7 collective-permute-start.2
  68.3 9.4 %collective-permute-start.5 = (bf16[512,896]{1,0:T(8,128)(2,1)S(1)}, bf16[512,896]{1,0:T(8,128)(2,1)S(1)}, u32[]{:S(2)}, u32[]{:S(2)}) collective-permute-start(bf16[512,896]{1,0:T(8,128)(2,1)S(1)} %collective-permute-done.2.far), channel_id=1, source_target_pairs={{0,1},{1,0},{2,3},{3,2},{4,5},{5,4},{6,7},{7,6},{8,9},{9,8},{10,11... | collective-permute-start | bytes 2752520 | tf_op jit(solution)/shard_map/ppermute | solution.py:25
  70.1 7.7 %collective-permute-start.6 = (bf16[512,896]{1,0:T(8,128)(2,1)S(1)}, bf16[512,896]{1,0:T(8,128)(2,1)S(1)}, u32[]{:S(2)}, u32[]{:S(2)}) collective-permute-start(bf16[512,896]{1,0:T(8,128)(2,1)S(1)} %collective-permute-done.near), channel_id=1, source_target_pairs={{0,1},{1,0},{2,3},{3,2},{4,5},{5,4},{6,7},{7,6},{8,9},{9,8},{10,11... | collective-permute-start | bytes 2752520 | tf_op jit(solution)/shard_map/ppermute | solution.py:25
  85.5 39.2 %collective-permute-start.7 = (bf16[1168,256]{1,0:T(8,128)(2,1)S(1)}, bf16[1168,256]{1,0:T(8,128)(2,1)S(1)}, u32[]{:S(2)}, u32[]{:S(2)}) collective-permute-start(bf16[1168,256]{1,0:T(8,128)(2,1)S(1)} %get-tuple-element.70), channel_id=1, source_target_pairs={{0,4},{1,5},{2,6},{3,7},{4,8},{5,9},{6,10},{7,11},{8,12},{9,13},{1... | collective-permute-start | bytes 1794056 | tf_op jit(solution)/shard_map/ppermute | solution.py:25
  86.8 37.9 %collective-permute-start.8 = (bf16[1168,256]{1,0:T(8,128)(2,1)S(1)}, bf16[1168,256]{1,0:T(8,128)(2,1)S(1)}, u32[]{:S(2)}, u32[]{:S(2)}) collective-permute-start(bf16[1168,256]{1,0:T(8,128)(2,1)S(1)} %get-tuple-element.71), channel_id=1, source_target_pairs={{0,12},{1,13},{2,14},{3,15},{4,0},{5,1},{6,2},{7,3},{8,4},{9,5},{1... | collective-permute-start | bytes 1794056 | tf_op jit(solution)/shard_map/ppermute | solution.py:25
  87.6 33.2 %collective-permute-start.9 = (bf16[128,1920]{1,0:T(8,128)(2,1)S(1)}, bf16[128,1920]{1,0:T(8,128)(2,1)S(1)}, u32[]{:S(2)}, u32[]{:S(2)}) collective-permute-start(bf16[128,1920]{1,0:T(8,128)(2,1)S(1)} %get-tuple-element.73), channel_id=1, source_target_pairs={{0,16},{1,17},{2,18},{3,19},{4,20},{5,21},{6,22},{7,23},{8,24},{9,... | collective-permute-start | bytes 1474568 | tf_op jit(solution)/shard_map/ppermute | solution.py:25
  99.0 25.7 %collective-permute-start.10 = (bf16[128,1920]{1,0:T(8,128)(2,1)S(1)}, bf16[128,1920]{1,0:T(8,128)(2,1)S(1)}, u32[]{:S(2)}, u32[]{:S(2)}) collective-permute-start(bf16[128,1920]{1,0:T(8,128)(2,1)S(1)} %get-tuple-element.74), channel_id=1, source_target_pairs={{0,48},{1,49},{2,50},{3,51},{4,52},{5,53},{6,54},{7,55},{8,56},{9,... | collective-permute-start | bytes 1474568 | tf_op jit(solution)/shard_map/ppermute | solution.py:25
  124.7 15.6 %collective-permute-start.12 = (bf16[1168,256]{1,0:T(8,128)(2,1)S(1)}, bf16[1168,256]{1,0:T(8,128)(2,1)S(1)}, u32[]{:S(2)}, u32[]{:S(2)}) collective-permute-start(bf16[1168,256]{1,0:T(8,128)(2,1)S(1)} %get-tuple-element.81), channel_id=1, source_target_pairs={{0,8},{1,9},{2,10},{3,11},{4,12},{5,13},{6,14},{7,15},{8,0},{9,1},... | collective-permute-start | bytes 1794056 | tf_op jit(solution)/shard_map/ppermute | solution.py:25
  126.4 17.9 %collective-permute-start.11 = (bf16[128,1920]{1,0:T(8,128)(2,1)S(1)}, bf16[128,1920]{1,0:T(8,128)(2,1)S(1)}, u32[]{:S(2)}, u32[]{:S(2)}) collective-permute-start(bf16[128,1920]{1,0:T(8,128)(2,1)S(1)} %get-tuple-element.76), channel_id=1, source_target_pairs={{0,32},{1,33},{2,34},{3,35},{4,36},{5,37},{6,38},{7,39},{8,40},{9,... | collective-permute-start | bytes 1474568 | tf_op jit(solution)/shard_map/ppermute | solution.py:25
  140.4 1.3 copy-start.2
  144.3 18.1 %collective-permute-start.13 = (bf16[400,128]{1,0:T(8,128)(2,1)S(1)}, bf16[400,128]{1,0:T(8,128)(2,1)S(1)}, u32[]{:S(2)}, u32[]{:S(2)}) collective-permute-start(bf16[400,128]{1,0:T(8,128)(2,1)S(1)} %get-tuple-element.91), channel_id=1, source_target_pairs={{0,2},{1,3},{2,16},{3,17},{4,6},{5,7},{6,20},{7,21},{8,10},{9,11},... | collective-permute-start | bytes 307208 | tf_op jit(solution)/shard_map/ppermute | solution.py:25
  144.4 21.2 %collective-permute-start.14 = (bf16[400,128]{1,0:T(8,128)(2,1)S(1)}, bf16[400,128]{1,0:T(8,128)(2,1)S(1)}, u32[]{:S(2)}, u32[]{:S(2)}) collective-permute-start(bf16[400,128]{1,0:T(8,128)(2,1)S(1)} %get-tuple-element.92), channel_id=1, source_target_pairs={{0,50},{1,51},{2,0},{3,1},{4,54},{5,55},{6,4},{7,5},{8,58},{9,59},... | collective-permute-start | bytes 307208 | tf_op jit(solution)/shard_map/ppermute | solution.py:25
  152.7 14.7 %collective-permute-start.15 = (bf16[400,128]{1,0:T(8,128)(2,1)S(1)}, bf16[400,128]{1,0:T(8,128)(2,1)S(1)}, u32[]{:S(2)}, u32[]{:S(2)}) collective-permute-start(bf16[400,128]{1,0:T(8,128)(2,1)S(1)} %get-tuple-element.93), channel_id=1, source_target_pairs={{0,16},{1,17},{2,18},{3,19},{4,20},{5,21},{6,22},{7,23},{8,24},{9,... | collective-permute-start | bytes 307208 | tf_op jit(solution)/shard_map/ppermute | solution.py:25
  160.6 37.6 %collective-permute-start.22 = (f32[112,512]{1,0:T(8,128)S(1)}, f32[112,512]{1,0:T(8,128)S(1)}, u32[]{:S(2)}, u32[]{:S(2)}) collective-permute-start(f32[112,512]{1,0:T(8,128)S(1)} %get-tuple-element.107), channel_id=1, source_target_pairs={{0,64},{1,65},{2,66},{3,67},{4,68},{5,69},{6,70},{7,71},{8,72},{9,... | collective-permute-start | bytes 688136 | tf_op jit(solution)/shard_map/ppermute | solution.py:25
  160.7 9.2 %collective-permute-start.16 = (bf16[400,128]{1,0:T(8,128)(2,1)S(1)}, bf16[400,128]{1,0:T(8,128)(2,1)S(1)}, u32[]{:S(2)}, u32[]{:S(2)}) collective-permute-start(bf16[400,128]{1,0:T(8,128)(2,1)S(1)} %get-tuple-element.94), channel_id=1, source_target_pairs={{0,48},{1,49},{2,50},{3,51},{4,52},{5,53},{6,54},{7,55},{8,56},{9,... | collective-permute-start | bytes 307208 | tf_op jit(solution)/shard_map/ppermute | solution.py:25
  162.4 11.9 %collective-permute-start.17 = (bf16[400,128]{1,0:T(8,128)(2,1)S(1)}, bf16[400,128]{1,0:T(8,128)(2,1)S(1)}, u32[]{:S(2)}, u32[]{:S(2)}) collective-permute-start(bf16[400,128]{1,0:T(8,128)(2,1)S(1)} %get-tuple-element.95), channel_id=1, source_target_pairs={{0,18},{1,19},{2,32},{3,33},{4,22},{5,23},{6,36},{7,37},{8,26},{9,... | collective-permute-start | bytes 307208 | tf_op jit(solution)/shard_map/ppermute | solution.py:25
  165.6 14.5 %collective-permute-start.18 = (bf16[400,128]{1,0:T(8,128)(2,1)S(1)}, bf16[400,128]{1,0:T(8,128)(2,1)S(1)}, u32[]{:S(2)}, u32[]{:S(2)}) collective-permute-start(bf16[400,128]{1,0:T(8,128)(2,1)S(1)} %get-tuple-element.96), channel_id=1, source_target_pairs={{0,34},{1,35},{2,48},{3,49},{4,38},{5,39},{6,52},{7,53},{8,42},{9,... | collective-permute-start | bytes 307208 | tf_op jit(solution)/shard_map/ppermute | solution.py:25
  167.5 12.5 %collective-permute-start.19 = (bf16[400,128]{1,0:T(8,128)(2,1)S(1)}, bf16[400,128]{1,0:T(8,128)(2,1)S(1)}, u32[]{:S(2)}, u32[]{:S(2)}) collective-permute-start(bf16[400,128]{1,0:T(8,128)(2,1)S(1)} %get-tuple-element.97), channel_id=1, source_target_pairs={{0,32},{1,33},{2,34},{3,35},{4,36},{5,37},{6,38},{7,39},{8,40},{9,... | collective-permute-start | bytes 307208 | tf_op jit(solution)/shard_map/ppermute | solution.py:25
  181.5 10.3 %collective-permute-start.20 = (f32[128,128]{1,0:T(8,128)S(1)}, f32[128,128]{1,0:T(8,128)S(1)}, u32[]{:S(2)}, u32[]{:S(2)}) collective-permute-start(f32[128,128]{1,0:T(8,128)S(1)} %get-tuple-element.100), channel_id=1, source_target_pairs={{0,1},{1,2},{2,3},{3,0},{4,16},{5,17},{6,18},{7,19},{8,32},{9,33},... | collective-permute-start | bytes 196616 | tf_op jit(solution)/shard_map/ppermute | solution.py:25
  186.0 11.0 %collective-permute-start.21 = (f32[128,128]{1,0:T(8,128)S(1)}, f32[128,128]{1,0:T(8,128)S(1)}, u32[]{:S(2)}, u32[]{:S(2)}) collective-permute-start(f32[128,128]{1,0:T(8,128)S(1)} %get-tuple-element.101), channel_id=1, source_target_pairs={{0,0},{1,1},{2,2},{3,3},{4,18},{5,19},{6,16},{7,17},{8,34},{9,35},... | collective-permute-start | bytes 196616 | tf_op jit(solution)/shard_map/ppermute | solution.py:25
